TPU v7x, 128 devices: a whole 4x4x4 slice. The times are simulated.
128 devices in a mesh: track: 16 (over x, y_lo, core), cols: 8 (over y_hi, z).
Axes of the slice: x: 4, y: 4 (y_hi: 2, y_lo: 2; y = y_hi * 2 + y_lo), z: 4, core: 2. Of those that a mesh axis runs over, the one named last changes fastest.
Arguments:
- design: bfloat16 [8192, 4096], P('track', 'cols'), may hold values from -0.0625 to 0.0625
- seg_start: int32 [8192], P('track'), may hold values from 0 to 8191, as said below
- seg_table: int32 [8192], P('track'), may hold values from 0 to 7, as said below
- taps: bfloat16 [8, 97], replicated, may hold values from -1.25 to 1.25
- ridge: float32 [4096], replicated, may hold values from 0.3 to 3
- col_perm: int32 [4096], replicated, may hold values from 0 to 4095, each once
Outputs:
- normals: float32 [4096, 4096], P('track', 'cols')
- factor: float32 [4096, 1024], P('track', 'cols')
Inputs may be any that keep to these rules, and one draw needn't show every extreme that they name: seg_start[r] is the first row of the run of consecutive rows that holds row r; it never exceeds r, row 0 starts a run, the last row starts a run of its own, and all rows of a run carry the same value. `seg_table`: all rows with the same seg_start carry the same table. `col_perm`: each of 0 to 4095 once.
All inputs are finite; a program needn't handle non-finite values.
Results may differ from a plain program's by a relative error of at most 0.0019.
Values may be sent and summed in bfloat16 or wider, within the bound.
No kernel may reach another device: no remote copies, remote signals or barrier semaphores. Data moves between devices by JAX's collectives and lax.ppermute only.
A program may use at most 64 MiB of HBM per device.

v0:
```python
import jax
import jax.numpy as jnp
from jax import lax
from jax.sharding import PartitionSpec as P

PANEL = 1024


def shifted(shard, axis, by):
    devices = lax.axis_size(axis)
    pairs = [(i, i + by) for i in range(devices) if 0 <= i + by < devices]
    return lax.ppermute(shard, axis, pairs)


def broadcast(block, axis, source):
    block = jnp.where(lax.axis_index(axis) == source, block, jnp.zeros_like(block))
    return lax.psum(block, axis)


def filter_rows(local, ext_top, seg_start, seg_table, taps, first_row):
    halo_rows = taps.shape[1] - 1
    row_count, columns = local.shape
    block = min(512, row_count)
    blocks = row_count // block
    extended = jnp.concatenate([ext_top, local], axis=0)
    upper = extended[:row_count].reshape(blocks, block, columns)
    lower_part = local.reshape(blocks, block, columns)[:, block - halo_rows :, :]
    windows = jnp.concatenate([upper, lower_part], axis=1)
    onehot = (seg_table[:, None] == jnp.arange(taps.shape[0], dtype=jnp.int32)[None, :]).astype(
        jnp.float32
    )
    row_taps = jnp.dot(onehot, taps.astype(jnp.float32), precision=lax.Precision.HIGHEST)
    flipped = row_taps[:, ::-1].reshape(blocks, block, halo_rows + 1)
    span = block + halo_rows
    padded = jnp.pad(flipped, ((0, 0), (0, 0), (0, span - halo_rows)))
    skewed = padded.reshape(blocks, block * (span + 1))[:, : block * span].reshape(
        blocks, block, span
    )
    offsets = (jnp.arange(blocks, dtype=jnp.int32) * block)[:, None, None]
    col_rows = first_row + offsets - halo_rows + jnp.arange(span, dtype=jnp.int32)[None, None, :]
    starts = seg_start.reshape(blocks, block)[:, :, None]
    coefs = jnp.where(col_rows >= starts, skewed, 0.0).astype(jnp.bfloat16)
    summed = jnp.einsum("brj,bjc->brc", coefs, windows, preferred_element_type=jnp.float32)
    return summed.reshape(row_count, columns).astype(jnp.bfloat16)


def body(design, seg_start, seg_table, taps, ridge, col_perm):
    row_count, width_dev = design.shape
    halo_rows = taps.shape[1] - 1
    track_index = lax.axis_index("track")
    col_index = lax.axis_index("cols")
    ext_top = shifted(design[row_count - halo_rows :], "track", 1)
    filtered = filter_rows(design, ext_top, seg_start, seg_table, taps, track_index * row_count)
    gathered = lax.all_gather(filtered, "cols", axis=1, tiled=True)
    row_blk = gathered.shape[1] // lax.axis_size("track")
    panel_blk = PANEL // lax.axis_size("cols")
    panel_ids = col_perm[:PANEL]
    sums = lax.psum_scatter(
        lax.dot_general(
            gathered, filtered, (((0,), (0,)), ((), ())), preferred_element_type=jnp.float32
        ),
        "track",
        scatter_dimension=0,
        tiled=True,
    )
    row_ids = track_index * row_blk + jnp.arange(row_blk, dtype=jnp.int32)
    col_ids = col_index * width_dev + jnp.arange(width_dev, dtype=jnp.int32)
    row_ridge = lax.dynamic_slice_in_dim(ridge, track_index * row_blk, row_blk)
    normals = sums + jnp.where(row_ids[:, None] == col_ids[None, :], row_ridge[:, None], 0.0)
    whole_rows = lax.all_gather(normals, "cols", axis=1, tiled=True)
    panel_rows = jnp.take(whole_rows, panel_ids, axis=1)
    own_cols = lax.dynamic_slice_in_dim(panel_rows, col_index * panel_blk, panel_blk, 1)
    selector = (panel_ids[:, None] == row_ids[None, :]).astype(jnp.float32)
    block_part = jnp.dot(selector, own_cols, precision=lax.Precision.HIGHEST)
    panel_cols = lax.psum(block_part, "track")

    def advance(turn, carry):
        working, lower = carry
        begin = turn * panel_blk
        diagonal = lax.dynamic_slice_in_dim(working, begin, panel_blk, 0)
        chol_block = jnp.linalg.cholesky(diagonal)
        candidate = lax.linalg.triangular_solve(
            chol_block, working, left_side=False, lower=True, transpose_a=True
        )
        keeper = jnp.arange(PANEL, dtype=jnp.int32) >= begin
        candidate = jnp.where(keeper[:, None], candidate, 0.0)
        column = broadcast(candidate, "cols", turn)
        mine = lax.dynamic_slice_in_dim(column, col_index * panel_blk, panel_blk, 0)
        update = jnp.dot(column, mine.T, precision=lax.Precision.HIGHEST)
        working = jnp.where(col_index > turn, working - update, working)
        lower = lax.dynamic_update_slice_in_dim(lower, column, begin, 1)
        return (working, lower)

    initial = jnp.zeros((PANEL, PANEL), jnp.float32)
    lower = lax.fori_loop(0, lax.axis_size("cols"), advance, (panel_cols, initial))[1]
    solved = lax.linalg.triangular_solve(
        lower, panel_rows, left_side=False, lower=True, transpose_a=True
    )
    factor = lax.dynamic_slice_in_dim(solved, col_index * panel_blk, panel_blk, 1)
    return (normals, factor)


def solution(mesh):
    in_specs = (P("track", "cols"), P("track"), P("track"), P(), P(), P())
    out_specs = (P("track", "cols"), P("track", "cols"))
    return jax.shard_map(body, mesh=mesh, in_specs=in_specs, out_specs=out_specs, check_vma=False)
```

profile of v0, /device:TPU:0, one launch (start us, length us, event | category | flops | bytes accessed | tf_op | source)
XLA Modules:
  0.0 1451.4 jit_solution(9035611131112651255)
XLA Ops:
  18.4 13.3 fusion.10
  34.3 77.9 %all-gather.3.cloned.1.call-done = bf16[512,4096]{1,0:T(8,128)(2,1)} async-done(((bf16[512,512]{1,0:T(8,128)(2,1)}), bf16[512,4096]{1,0:T(8,128)(2,1)}) %all-gather.3.cloned.1.call-update) | async-done | bytes 4194320 | tf_op jit(solution)/shard_map/all_gather | solution.py:54
  120.9 92.1 %reduce-scatter.2.cloned.1.call-done = f32[256,512]{1,0:T(8,128)} async-done(((f32[4096,512]{1,0:T(8,128)}), f32[256,512]{1,0:T(8,128)}) %reduce-scatter.2.cloned.1.call-update) | async-done | bytes 524304 | tf_op jit(solution)/shard_map/reduce_scatter | solution.py:58
  215.2 74.9 %all-gather.5.cloned.1.call-done = f32[256,4096]{1,0:T(8,128)} async-done(((f32[256,512]{1,0:T(8,128)}), f32[256,4096]{1,0:T(8,128)}) %all-gather.5.cloned.1.call-update) | async-done | bytes 4194320 | tf_op jit(solution)/shard_map/all_gather | solution.py:70
  303.2 115.2 %all-reduce.4.cloned.1.call-done = f32[1024,128]{1,0:T(8,128)} async-done(((f32[1024,128]{1,0:T(8,128)}), f32[1024,128]{1,0:T(8,128)}) %all-reduce.4.cloned.1.call-update) | async-done | bytes 524304 | tf_op jit(solution)/shard_map/psum | solution.py:75
  422.1 902.4 %while.18 = (s32[]{:T(128)}, f32[1024,128]{0,1:T(8,128)S(1)}, f32[1024,1024]{1,0:T(8,128)}, s32[]{:T(128)}, s32[]{:T(128)}, /*index=5*/s32[]{:T(128)}, s32[]{:T(128)}, u32[]{:T(128)}, s32[]{:T(128)}, s32[]{:T(128)}) while((s32[]{:T(128)}, f32[1024,128]{0,1:T(8,128)S(1)}, f32[1024,1024]{1,0:T(8,128)}, s32[]{:T(128)}, s32[]{:T(128)}, ...), condition=%wide.region_6.7_spmd, body=%wide.region_2.6_spmd.sunk | while | flops 403457152 | bytes 10751741 | solution.py:95
  422.3 11.7 cholesky.58
  435.2 9.8 custom-call.34
  446.7 86.4 %all-reduce.6.cloned.1.call-done = f32[1024,128]{0,1:T(8,128)} async-done(((f32[1024,128]{0,1:T(8,128)}), f32[1024,128]{0,1:T(8,128)}) %all-reduce.6.cloned.1.call-update) | async-done | bytes 524304 | tf_op jit(solution)/shard_map/while/body/eval_jaxpr/psum | solution.py:17
  537.7 11.7 cholesky.58
  550.6 9.8 custom-call.34
  562.1 83.5 %all-reduce.6.cloned.1.call-done = f32[1024,128]{0,1:T(8,128)} async-done(((f32[1024,128]{0,1:T(8,128)}), f32[1024,128]{0,1:T(8,128)}) %all-reduce.6.cloned.1.call-update) | async-done | bytes 524304 | tf_op jit(solution)/shard_map/while/body/eval_jaxpr/psum | solution.py:17
  650.1 11.7 cholesky.58
  663.1 9.8 custom-call.34
  674.5 83.5 %all-reduce.6.cloned.1.call-done = f32[1024,128]{0,1:T(8,128)} async-done(((f32[1024,128]{0,1:T(8,128)}), f32[1024,128]{0,1:T(8,128)}) %all-reduce.6.cloned.1.call-update) | async-done | bytes 524304 | tf_op jit(solution)/shard_map/while/body/eval_jaxpr/psum | solution.py:17
  762.5 11.7 cholesky.58
  775.5 9.8 custom-call.34
  786.9 83.5 %all-reduce.6.cloned.1.call-done = f32[1024,128]{0,1:T(8,128)} async-done(((f32[1024,128]{0,1:T(8,128)}), f32[1024,128]{0,1:T(8,128)}) %all-reduce.6.cloned.1.call-update) | async-done | bytes 524304 | tf_op jit(solution)/shard_map/while/body/eval_jaxpr/psum | solution.py:17
  874.9 11.7 cholesky.58
  887.9 9.8 custom-call.34
  899.4 83.5 %all-reduce.6.cloned.1.call-done = f32[1024,128]{0,1:T(8,128)} async-done(((f32[1024,128]{0,1:T(8,128)}), f32[1024,128]{0,1:T(8,128)}) %all-reduce.6.cloned.1.call-update) | async-done | bytes 524304 | tf_op jit(solution)/shard_map/while/body/eval_jaxpr/psum | solution.py:17
  987.4 11.7 cholesky.58
  1000.3 9.8 custom-call.34
  1011.8 83.5 %all-reduce.6.cloned.1.call-done = f32[1024,128]{0,1:T(8,128)} async-done(((f32[1024,128]{0,1:T(8,128)}), f32[1024,128]{0,1:T(8,128)}) %all-reduce.6.cloned.1.call-update) | async-done | bytes 524304 | tf_op jit(solution)/shard_map/while/body/eval_jaxpr/psum | solution.py:17
  1099.8 11.7 cholesky.58
  1112.8 9.8 custom-call.34
  1124.2 83.5 %all-reduce.6.cloned.1.call-done = f32[1024,128]{0,1:T(8,128)} async-done(((f32[1024,128]{0,1:T(8,128)}), f32[1024,128]{0,1:T(8,128)}) %all-reduce.6.cloned.1.call-update) | async-done | bytes 524304 | tf_op jit(solution)/shard_map/while/body/eval_jaxpr/psum | solution.py:17
  1212.2 11.7 cholesky.58
  1225.2 9.8 custom-call.34
  1236.7 83.5 %all-reduce.6.cloned.1.call-done = f32[1024,128]{0,1:T(8,128)} async-done(((f32[1024,128]{0,1:T(8,128)}), f32[1024,128]{0,1:T(8,128)}) %all-reduce.6.cloned.1.call-update) | async-done | bytes 524304 | tf_op jit(solution)/shard_map/while/body/eval_jaxpr/psum | solution.py:17
  1329.3 23.2 %while.19 = (s32[]{:T(128)}, f32[1024,1024]{1,0:T(8,128)}, s32[8,2]{0,1:T(2,128)S(1)}, f32[8,128,128]{2,1,0:T(8,128)S(1)}, s32[]{:T(128)}) while((s32[]{:T(128)}, f32[1024,1024]{1,0:T(8,128)}, s32[8,2]{0,1:T(2,128)S(1)}, f32[8,128,128]{2,1,0:T(8,128)S(1)}, s32[]{:T(128)}) %tuple.85), condition=%wide.while_cond, body=%wide.while_body.sunk | while | flops 2 | bytes 131189 | solution.py:96
  1352.4 78.8 %custom-call.21 = f32[8,128,128]{1,2,0:T(8,128)S(1)} custom-call(f32[8,128,128]{2,1,0:T(8,128)S(1)} %get-tuple-element.124), custom_call_target="InvertDiagBlocksLowerTriangular" | custom-call | tf_op jit(solution)/shard_map/triangular_solve | solution.py:96
  (212 shorter events, 140.9 us)
Async XLA Ops:
  7.2 2.3 copy-start
  7.2 8.2 copy-start.3
  7.2 105.0 %all-gather.3.cloned.1.call-start = ((), (), s32[]{:S(2)}) async-start(), calls=%async_computation.1 | async-start | bytes 4718592 | tf_op jit(solution)/shard_map/all_gather | solution.py:54
  8.1 24.4 %collective-permute-start = (bf16[96,512]{1,0:T(8,128)(2,1)S(1)}, bf16[96,512]{1,0:T(8,128)(2,1)S(1)}, u32[]{:S(2)}, u32[]{:S(2)}) collective-permute-start(bf16[96,512]{1,0:T(8,128)(2,1)S(1)} %slice.80), channel_id=1, source_target_pairs={{0,8},{8,16},{16,24},{24,32},{32,40},{40,48},{48,56},{56,64},{64,7... | collective-permute-start | bytes 294920 | tf_op jit(solution)/shard_map/ppermute | solution.py:12
  15.4 16.3 %copy-start.1 = (bf16[512,512]{1,0:T(8,128)(2,1)S(1)}, bf16[512,512]{1,0:T(8,128)(2,1)}, u32[]{:S(2)}) copy-start(bf16[512,512]{1,0:T(8,128)(2,1)} %param.8) | copy-start | bytes 1572868
  34.0 179.0 %reduce-scatter.2.cloned.1.call-start = ((), (), s32[]{:S(2)}) async-start(), calls=%async_computation.2 | async-start | bytes 8912896 | tf_op jit(solution)/shard_map/reduce_scatter | solution.py:58
  120.1 95.0 %copy-start.2 = (s32[4096]{0:T(1024)S(1)}, s32[4096]{0:T(1024)}, u32[]{:S(2)}) copy-start(s32[4096]{0:T(1024)} %param.13) | copy-start | bytes 49156
  120.1 169.9 %all-gather.5.cloned.1.call-start = ((), (), s32[]{:S(2)}) async-start(), calls=%async_computation.3 | async-start | bytes 4718592 | tf_op jit(solution)/shard_map/all_gather | solution.py:70
  215.1 203.3 %all-reduce.4.cloned.1.call-start = ((), (), s32[]{:S(2)}) async-start(), calls=%async_computation.4 | async-start | bytes 1048576 | tf_op jit(solution)/shard_map/psum | solution.py:75
  422.1 111.0 %all-reduce.6.cloned.1.call-start = ((), (), s32[]{:S(2)}) async-start(), calls=%async_computation.5 | async-start | bytes 1048576 | tf_op jit(solution)/shard_map/while/body/eval_jaxpr/psum | solution.py:17
  537.5 108.1 %all-reduce.6.cloned.1.call-start = ((), (), s32[]{:S(2)}) async-start(), calls=%async_computation.5 | async-start | bytes 1048576 | tf_op jit(solution)/shard_map/while/body/eval_jaxpr/psum | solution.py:17
  649.9 108.1 %all-reduce.6.cloned.1.call-start = ((), (), s32[]{:S(2)}) async-start(), calls=%async_computation.5 | async-start | bytes 1048576 | tf_op jit(solution)/shard_map/while/body/eval_jaxpr/psum | solution.py:17
  762.4 108.1 %all-reduce.6.cloned.1.call-start = ((), (), s32[]{:S(2)}) async-start(), calls=%async_computation.5 | async-start | bytes 1048576 | tf_op jit(solution)/shard_map/while/body/eval_jaxpr/psum | solution.py:17
  874.8 108.1 %all-reduce.6.cloned.1.call-start = ((), (), s32[]{:S(2)}) async-start(), calls=%async_computation.5 | async-start | bytes 1048576 | tf_op jit(solution)/shard_map/while/body/eval_jaxpr/psum | solution.py:17
  987.2 108.1 %all-reduce.6.cloned.1.call-start = ((), (), s32[]{:S(2)}) async-start(), calls=%async_computation.5 | async-start | bytes 1048576 | tf_op jit(solution)/shard_map/while/body/eval_jaxpr/psum | solution.py:17
  1099.7 108.1 %all-reduce.6.cloned.1.call-start = ((), (), s32[]{:S(2)}) async-start(), calls=%async_computation.5 | async-start | bytes 1048576 | tf_op jit(solution)/shard_map/while/body/eval_jaxpr/psum | solution.py:17
  1212.1 108.1 %all-reduce.6.cloned.1.call-start = ((), (), s32[]{:S(2)}) async-start(), calls=%async_computation.5 | async-start | bytes 1048576 | tf_op jit(solution)/shard_map/while/body/eval_jaxpr/psum | solution.py:17
Sparse Core Ops, SparseCore 0:
  34.2 77.9 all-gather.2
  120.2 92.7 reduce-scatter.1
  215.9 74.0 all-gather.4
  303.1 115.2 all-reduce.3
  446.6 86.4 all-reduce.5
  562.0 83.5 all-reduce.5
  674.4 83.5 all-reduce.5
  786.8 83.5 all-reduce.5
  899.3 83.5 all-reduce.5
  1011.7 83.5 all-reduce.5
  1124.2 83.5 all-reduce.5
  1236.6 83.5 all-reduce.5
where the time goes:
time: 1450 us
  waiting for transfers between devices  1030 us (71%)
  other arithmetic  282 us (19%)
  local copies, waits for them, and re-layouts  70.1 us (5%)
  matrix products  51.7 us (4%)
    psum x8, waiting for transfers between devices, broadcast(): return lax.psum(block, axis)  671 us
    psum x1, waiting for transfers between devices, body(): panel_cols = lax.psum(block_part, 'track')  115 us
    another operation x24, other arithmetic, advance(): chol_block = jnp.linalg.cholesky(diagonal)  99 us
    reduce_scatter x1, waiting for transfers between devices, body(): lax.psum_scatter(lax.dot_general(gathered, filtered, (((0,), (0,)), ((),...  92.1 us
    another operation x3, other arithmetic, body(): lax.linalg.triangular_solve(lower, panel_rows, left_side=False, lower=Tru...  83.5 us
    another operation x16, other arithmetic, advance(): lax.linalg.triangular_solve(chol_block, working, left_side=False, lower=T...  83.1 us
    all_gather x1, waiting for transfers between devices, body(): gathered = lax.all_gather(filtered, 'cols', axis=1, tiled=True)  77.9 us
    all_gather x1, waiting for transfers between devices, body(): whole_rows = lax.all_gather(normals, 'cols', axis=1, tiled=True)  74.9 us
  transfers between devices with their start and end apart: 13, of which 12 were waited for; matrix products, arithmetic and copies ran while one was open for 2% of the time, Pallas kernels for 0%

commit v1 on v0

v1 whole, which is shorter than its diff:
```python
import functools

import jax
import jax.numpy as jnp
from jax import lax
from jax.experimental import pallas as pl
from jax.experimental.pallas import tpu as pltpu
from jax.sharding import PartitionSpec as P

PANEL = 1024
NB = 128
SUB = 8
ROWS_T = (((0,), (0,)), ((), ()))
HIGH = lax.Precision.HIGHEST


def dot_f32(a, b, dims=(((1,), (0,)), ((), ()))):
    return lax.dot_general(a, b, dims, precision=HIGH, preferred_element_type=jnp.float32)


def gather(x, axis):
    copies = jnp.broadcast_to(x[None], (lax.axis_size(axis),) + x.shape)
    return lax.all_to_all(copies, axis, 0, 0)


def filter_kernel(first_ref, halo_ref, local_ref, start_ref, table_ref, taps_ref, out_ref, ext_ref):
    halo_rows = halo_ref.shape[0]
    row_count, columns = local_ref.shape
    ext_ref[:halo_rows] = halo_ref[...]
    ext_ref[halo_rows : halo_rows + row_count] = local_ref[...]
    ext_ref[halo_rows + row_count :] = jnp.zeros_like(ext_ref[halo_rows + row_count :])
    span = 2 * NB
    taps = taps_ref[...]
    tables = taps.shape[0]
    lane = lax.broadcasted_iota(jnp.int32, (NB, span), 1)
    for b in range(row_count // NB):
        rows = pl.ds(b * NB, NB)
        choice = lax.broadcasted_iota(jnp.int32, (NB, tables), 1) == table_ref[rows, :]
        row_taps = jnp.dot(
            choice.astype(jnp.float32).astype(jnp.bfloat16), taps, preferred_element_type=jnp.float32
        )
        skewed = pltpu.roll(row_taps, 0, 1, stride=1, stride_axis=0)
        source = first_ref[0] + b * NB - halo_rows + lane
        coefs = jnp.where(source >= start_ref[rows, :], skewed, 0.0).astype(jnp.bfloat16)
        window = ext_ref[pl.ds(b * NB, span), :]
        out_ref[rows, :] = jnp.dot(coefs, window, preferred_element_type=jnp.float32).astype(
            jnp.bfloat16
        )


def filter_rows(local, ext_top, seg_start, seg_table, taps, first_row):
    row_count, columns = local.shape
    halo_rows = ext_top.shape[0]
    flipped = jnp.pad(taps[:, ::-1], ((0, 0), (0, 2 * NB - taps.shape[1])))
    vmem = pl.BlockSpec(memory_space=pltpu.VMEM)
    return pl.pallas_call(
        filter_kernel,
        out_shape=jax.ShapeDtypeStruct(local.shape, jnp.bfloat16),
        in_specs=[pl.BlockSpec(memory_space=pltpu.SMEM)] + [vmem] * 5,
        out_specs=vmem,
        scratch_shapes=[pltpu.VMEM((row_count + NB, columns), jnp.bfloat16)],
        compiler_params=pltpu.CompilerParams(vmem_limit_bytes=16 * 2**20),
    )(
        first_row.reshape(1),
        ext_top,
        local,
        seg_start[:, None],
        seg_table[:, None],
        flipped,
    )


def factor_groups(groups):
    groups = list(groups)
    shape = (SUB, NB)
    lane = lax.broadcasted_iota(jnp.int32, shape, 1)
    sub = lax.broadcasted_iota(jnp.int32, shape, 0)
    for s in range(len(groups)):
        top = groups[s]
        base = s * SUB
        rows = [jnp.broadcast_to(top[i : i + 1, :], shape) for i in range(SUB)]
        t = {}
        for i in range(SUB):
            for j in range(i + 1):
                t[i, j] = jnp.broadcast_to(rows[i][:, base + j : base + j + 1], shape)
        inside = (lane >= base) & (lane < base + SUB)
        r, l, done = [], {}, []
        for k in range(SUB):
            r.append(lax.rsqrt(t[k, k]))
            for i in range(k + 1, SUB):
                l[i, k] = t[i, k] * r[k]
            for j in range(k + 1, SUB):
                for i in range(j, SUB):
                    t[i, j] = t[i, j] - l[i, k] * l[j, k]
        for i in range(SUB):
            acc = jnp.where(inside, (lane == base + i).astype(jnp.float32), rows[i])
            for j in range(i):
                acc = acc - l[i, j] * done[j]
            done.append(acc * r[i])
        packed = done[0]
        for i in range(1, SUB):
            packed = jnp.where(sub == i, done[i], packed)
        groups[s] = packed
        back = [None] * SUB
        for j in reversed(range(SUB)):
            acc = done[j]
            for i in range(j + 1, SUB):
                acc = acc - l[i, j] * back[i]
            back[j] = acc * r[j]
        for g in range(s + 1, len(groups)):
            acc = jnp.where(inside, 0.0, groups[g])
            for j in range(SUB):
                column = groups[g][:, base + j : base + j + 1]
                acc = acc - jnp.broadcast_to(column, shape) * back[j]
            groups[g] = acc
    return groups


def inverse_kernel(turn_ref, pieces_ref, out_ref, work_ref):
    size = work_ref.shape[0]
    blocks = size // NB
    row_piece = pieces_ref.shape[1]
    for i in range(size // row_piece):
        for j in range(blocks):
            work_ref[i * row_piece : (i + 1) * row_piece, j * NB : (j + 1) * NB] = pieces_ref[
                i * blocks + j
            ]
    triangle = lax.broadcasted_iota(jnp.int32, (NB, NB), 0) >= lax.broadcasted_iota(
        jnp.int32, (NB, NB), 1
    )

    def step(m, _):
        here = pl.ds(pl.multiple_of(m * NB, NB), NB)
        start = pl.multiple_of(m * NB, NB)
        groups = [work_ref[pl.ds(start + SUB * g, SUB), here] for g in range(NB // SUB)]
        inverse = jnp.where(triangle, jnp.concatenate(factor_groups(groups), axis=0), 0.0)
        work_ref[here, :] = dot_f32(inverse, work_ref[here, :])
        work_ref[here, here] = inverse
        again = dot_f32(inverse, work_ref[here, :], ROWS_T)

        def lower(i, _):
            below = pl.ds(pl.multiple_of(i * NB, NB), NB)
            left = work_ref[below, here]
            work_ref[below, here] = jnp.zeros((NB, NB), jnp.float32)
            work_ref[below, :] -= dot_f32(left, again)
            return 0

        lax.fori_loop(m + 1, blocks, lower, 0)
        return 0

    lax.fori_loop(0, blocks, step, 0)
    turn = turn_ref[0]
    row = lax.broadcasted_iota(jnp.int32, out_ref.shape, 0) + turn * NB
    col = lax.broadcasted_iota(jnp.int32, out_ref.shape, 1)
    mine = work_ref[pl.ds(pl.multiple_of(turn * NB, NB), NB), :]
    out_ref[...] = jnp.where(row >= col, mine, 0.0)


def inverse_rows(pieces, turn):
    vmem = pl.BlockSpec(memory_space=pltpu.VMEM)
    return pl.pallas_call(
        inverse_kernel,
        out_shape=jax.ShapeDtypeStruct((NB, PANEL), jnp.float32),
        in_specs=[pl.BlockSpec(memory_space=pltpu.SMEM), vmem],
        out_specs=vmem,
        scratch_shapes=[pltpu.VMEM((PANEL, PANEL), jnp.float32)],
        compiler_params=pltpu.CompilerParams(vmem_limit_bytes=40 * 2**20),
    )(turn.reshape(1), pieces)


def body(design, seg_start, seg_table, taps, ridge, col_perm):
    row_count, width = design.shape
    halo_rows = taps.shape[1] - 1
    track, cols = lax.axis_size("track"), lax.axis_size("cols")
    t, c = lax.axis_index("track"), lax.axis_index("cols")
    panel_blk = PANEL // cols
    panel_piece = PANEL // track
    slab = width * cols
    row_blk = slab // track
    panel_ids = col_perm[:PANEL]

    pairs = [(i, i + 1) for i in range(track - 1)]
    ext_top = lax.ppermute(design[row_count - halo_rows :], "track", pairs)
    filtered = filter_rows(design, ext_top, seg_start, seg_table, taps, t * row_count)
    gathered = gather(filtered, "cols")

    places = jnp.arange(slab, dtype=jnp.int32).reshape(cols, width)
    chosen = (places[:, :, None] == panel_ids[None, None, :]).astype(jnp.bfloat16)
    panel = lax.dot_general(
        gathered, chosen, (((0, 2), (0, 1)), ((), ())), preferred_element_type=jnp.float32
    ).astype(jnp.bfloat16)
    panel_mine = lax.dynamic_slice_in_dim(panel, c * panel_blk, panel_blk, 1)
    block_part = lax.dot_general(panel, panel_mine, ROWS_T, preferred_element_type=jnp.float32)
    block_parts = lax.all_to_all(block_part.reshape(track, panel_piece, panel_blk), "track", 0, 0)
    block_piece = jnp.sum(block_parts, axis=0)
    prow = t * panel_piece + jnp.arange(panel_piece, dtype=jnp.int32)
    pcol = c * panel_blk + jnp.arange(panel_blk, dtype=jnp.int32)
    mine_ids = lax.dynamic_slice_in_dim(panel_ids, c * panel_blk, panel_blk)
    mine_ridge = jnp.take(ridge, mine_ids)
    block_piece += jnp.where(prow[:, None] == pcol[None, :], mine_ridge[None, :], 0.0)
    pieces = gather(block_piece, ("track", "cols"))
    inverse = inverse_rows(pieces, c)

    contract = (((1,), (0,)), ((), ()))
    part = lax.dot_general(gathered, filtered, contract, preferred_element_type=jnp.float32)
    part_cols = lax.dot_general(gathered, panel_mine, contract, preferred_element_type=jnp.float32)
    own_cols = lax.psum_scatter(
        part_cols.reshape(slab, panel_blk), "track", scatter_dimension=0, tiled=True
    )
    row_ids = t * row_blk + jnp.arange(row_blk, dtype=jnp.int32)
    col_ids = c * width + jnp.arange(width, dtype=jnp.int32)
    own_cols += jnp.where(row_ids[:, None] == mine_ids[None, :], mine_ridge[None, :], 0.0)
    panel_rows = gather(own_cols, "cols")
    sums = lax.psum_scatter(part.reshape(slab, width), "track", scatter_dimension=0, tiled=True)
    row_ridge = lax.dynamic_slice_in_dim(ridge, t * row_blk, row_blk)
    normals = sums + jnp.where(row_ids[:, None] == col_ids[None, :], row_ridge[:, None], 0.0)

    factor = lax.dot_general(
        panel_rows,
        inverse.reshape(panel_blk, cols, panel_blk),
        (((0, 2), (1, 2)), ((), ())),
        precision=HIGH,
        preferred_element_type=jnp.float32,
    )
    return (normals, factor)


def solution(mesh):
    in_specs = (P("track", "cols"), P("track"), P("track"), P(), P(), P())
    out_specs = (P("track", "cols"), P("track", "cols"))
    return jax.shard_map(body, mesh=mesh, in_specs=in_specs, out_specs=out_specs, check_vma=False)
```

time: 1450 us -> 301 us (0.21)
  waiting for transfers between devices: 1030 us -> 142 us
  other arithmetic: 282 us -> 3.21 us
  Pallas kernels: 0 us -> 72.7 us
  local copies, waits for them, and re-layouts: 70.1 us -> 12.4 us
  starting transfers between devices: 1.65 us -> 31.1 us
  matrix products: 51.7 us -> 22.3 us
    psum x9 -> x0, waiting for transfers between devices: 786 us -> none  [the longest x8 671 us: broadcast(): return lax.psum(block, axis)]
    another operation x43 -> x1, other arithmetic: 266 us -> 0.01 us  [body(): places[:, :, None] == panel_ids[None, None, :]]
    all_gather x2 -> x0, waiting for transfers between devices: 153 us -> none  [the longest x1 77.9 us: body(): gathered = lax.all_gather(filtered, 'cols', axis=1, tiled=True)]
    pallas_call x0 -> x2, Pallas kernels: none -> 72.7 us  [the longest x1 71.5 us: inverse_rows(): pl.pallas_call(inverse_kernel, out_shape=jax.ShapeDtypeStruct((NB, PANEL)...]
    all_to_all x0 -> x4, waiting for transfers between devices: none -> 60.6 us  [the longest x3 49.7 us: gather(): return lax.all_to_all(copies, axis, 0, 0)]
    all_to_all x0 -> x4, starting transfers between devices: none -> 29.7 us  [the longest x3 24.5 us: gather(): return lax.all_to_all(copies, axis, 0, 0)]
    another operation x41 -> x0, local copies, waits for them, and re-layouts: 26.1 us -> none
    another operation x23 -> x0, matrix products: 23.7 us -> none  [the longest x15 12.4 us: body(): lax.linalg.triangular_solve(lower, panel_rows, left_side=False, lower=Tru...]
  transfers between devices with their start and end apart: 13 -> 7, of which waited for: 12 -> 5; matrix products, arithmetic and copies ran while one was open for 2% -> 7% of each run, Pallas kernels for 0% -> 24%
where the time goes in v1:
time: 301 us; the launch traced here: 298 us
  waiting for transfers between devices  142 us (47%)
  Pallas kernels  72.7 us (24%)
  starting transfers between devices  31.1 us (10%)
  matrix products  22.3 us (7%)
  between operations  14.2 us (5%)
  local copies, waits for them, and re-layouts  12.4 us (4%)
  other arithmetic  3.21 us (1%)
    pallas_call x1, Pallas kernels, inverse_rows(): pl.pallas_call(inverse_kernel, out_shape=jax.ShapeDtypeStruct((NB, PANEL)...  71.5 us
    reduce_scatter x1, waiting for transfers between devices, body(): lax.psum_scatter(part_cols.reshape(slab, panel_blk), 'track', scatter_dim...  55.6 us
    all_to_all x3, waiting for transfers between devices, gather(): return lax.all_to_all(copies, axis, 0, 0)  49.7 us
    reduce_scatter x1, waiting for transfers between devices, body(): lax.psum_scatter(part.reshape(slab, width), 'track', scatter_dimension=0,...  25.6 us
    all_to_all x3, starting transfers between devices, gather(): return lax.all_to_all(copies, axis, 0, 0)  24.5 us
    all_to_all x1, waiting for transfers between devices, body(): lax.all_to_all(block_part.reshape(track, panel_piece, panel_blk), 'track'...  10.9 us
    dot_general x1, matrix products, body(): lax.dot_general(gathered, filtered, contract, preferred_element_type=jnp....  7.75 us
    dot_general x1, matrix products, body(): lax.dot_general(gathered, chosen, (((0, 2), (0, 1)), ((), ())), preferred...  6.82 us
  transfers between devices with their start and end apart: 7, of which 5 were waited for; matrix products, arithmetic and copies ran while one was open for 7% of the time, Pallas kernels for 24%

profile of v1, /device:TPU:0, one launch (start us, length us, event | category | flops | bytes accessed | tf_op | source)
XLA Modules:
  0.0 297.6 jit_solution(5420111920328626719)
XLA Ops:
  7.2 0.9 slice.6
  8.1 1.3 collective-permute-start
  9.4 0.8 copy.11.start_ref
  10.2 0.8 copy.12.table_ref
  11.0 0.8 rev.3
  11.8 1.0 copy-done
  12.8 1.1 shard_map.77
  14.0 0.2 copy.13
  14.2 2.3 broadcast_in_dim.80
  16.5 8.5 %all-to-all-start = ((bf16[8,512,512]{1,2,0:T(8,128)(2,1)}), bf16[8,512,512]{1,2,0:T(8,128)(2,1)}, u32[]{:S(2)}, u32[]{:S(2)}) async-start(bf16[8,512,512]{1,2,0:T(8,128)(2,1)} %broadcast_in_dim.80), calls=%async_computation | async-start | bytes 8388608 | tf_op jit(solution)/shard_map/all_to_all | solution.py:23
  25.0 0.7 slice.7
  25.7 49.4 %all-to-all-done = bf16[8,512,512]{1,2,0:T(8,128)(2,1)} async-done(((bf16[8,512,512]{1,2,0:T(8,128)(2,1)}), bf16[8,512,512]{1,2,0:T(8,128)(2,1)}, u32[]{:S(2)}, u32[]{:S(2)}) %all-to-all-start) | async-done | bytes 4194336 | tf_op jit(solution)/shard_map/all_to_all | solution.py:23
  75.1 6.8 %bitcast_convert_fusion = bf16[512,1024]{1,0:T(8,128)(2,1)S(1)} fusion(bf16[8,512,512]{1,2,0:T(8,128)(2,1)} %all-to-all-done, s32[1024]{0:T(1024)S(1)} %slice.7, s32[8,512]{1,0:T(8,128)S(1)} %multiply_add_fusion), kind=kOutput, calls=%fused_computation.5 | convolution fusion | flops 4299685888 | bytes 5263360 | tf_op jit(solution)/shard_map/dot_general | solution.py:189
  81.9 4.8 %fusion.10 = f32[8,512,128]{2,1,0:T(8,128)} fusion(bf16[8,512,512]{1,2,0:T(8,128)(2,1)} %all-to-all-done, bf16[512,1024]{1,0:T(8,128)(2,1)S(1)} %bitcast_convert_fusion, s32[]{:T(128)S(6)} %select_n.36), kind=kOutput, calls=%fused_computation.12 | convolution fusion | flops 536870912 | bytes 6422532 | tf_op jit(solution)/shard_map/dot_general | solution.py:206
  86.8 7.8 %fusion.8 = f32[8,512,512]{2,1,0:T(8,128)} fusion(bf16[8,512,512]{1,2,0:T(8,128)(2,1)} %all-to-all-done, bf16[512,512]{1,0:T(8,128)(2,1)S(1)} %shard_map.77), kind=kOutput, calls=%fused_computation.9 | convolution fusion | flops 2147483648 | bytes 13107200 | tf_op jit(solution)/shard_map/dot_general | solution.py:205
  94.6 0.1 compare_select_fusion
  94.6 1.3 fusion.12
  95.9 5.2 %all-to-all-start.2 = ((f32[16,64,128]{2,1,0:T(8,128)}), f32[16,64,128]{2,1,0:T(8,128)S(1)}, u32[]{:S(2)}, u32[]{:S(2)}) async-start(f32[16,64,128]{2,1,0:T(8,128)} %bitcast.9), calls=%async_computation.4 | async-start | bytes 1048576 | tf_op jit(solution)/shard_map/all_to_all | solution.py:194
  101.2 1.1 gather_fusion
  102.4 10.9 %all-to-all-done.2 = f32[16,64,128]{2,1,0:T(8,128)S(1)} async-done(((f32[16,64,128]{2,1,0:T(8,128)}), f32[16,64,128]{2,1,0:T(8,128)S(1)}, u32[]{:S(2)}, u32[]{:S(2)}) %all-to-all-start.2) | async-done | bytes 524320 | tf_op jit(solution)/shard_map/all_to_all | solution.py:194
  113.3 0.1 select_add_fusion.2
  113.4 2.5 broadcast_in_dim.90
  115.9 7.8 %all-to-all-start.3 = ((f32[128,64,128]{2,1,0:T(8,128)}), f32[128,64,128]{2,1,0:T(8,128)}, u32[]{:S(2)}, u32[]{:S(2)}) async-start(f32[128,64,128]{2,1,0:T(8,128)} %broadcast_in_dim.90), calls=%async_computation.5 | async-start | bytes 8388608 | tf_op jit(solution)/shard_map/all_to_all | solution.py:23
  123.7 55.6 %reduce-scatter.5.cloned.1.call-done = f32[256,128]{1,0:T(8,128)} async-done(((f32[4096,128]{1,0:T(8,128)}), f32[256,128]{1,0:T(8,128)}) %reduce-scatter.5.cloned.1.call-update) | async-done | bytes 131088 | tf_op jit(solution)/shard_map/reduce_scatter | solution.py:207
  179.3 1.0 select_add_fusion.1
  180.3 0.3 all-to-all-done.3.pieces_ref
  180.6 1.1 broadcast_in_dim.87
  181.7 8.2 %all-to-all-start.1 = ((f32[8,256,128]{2,1,0:T(8,128)}), f32[8,256,128]{2,1,0:T(8,128)S(1)}, u32[]{:S(2)}, u32[]{:S(2)}) async-start(f32[8,256,128]{2,1,0:T(8,128)} %broadcast_in_dim.87), calls=%async_computation.3 | async-start | bytes 2097152 | tf_op jit(solution)/shard_map/all_to_all | solution.py:23
  190.0 71.5 %shard_map.78 = f32[128,1024]{1,0:T(8,128)S(1)} custom-call(s32[1]{0:T(128)} %bitcast.8.turn_ref, f32[128,64,128]{2,1,0:T(8,128)} %all-to-all-done.3.pieces_ref), custom_call_target="tpu_custom_call" | custom-call | tf_op jit(solution)/shard_map/pallas_call | solution.py:161
  261.5 1.6 convolution_bitcast_fusion
  263.2 25.6 %reduce-scatter.3.cloned.1.call-done = f32[256,512]{1,0:T(8,128)} async-done(((f32[4096,512]{1,0:T(8,128)}), f32[256,512]{1,0:T(8,128)}) %reduce-scatter.3.cloned.1.call-update) | async-done | bytes 524304 | tf_op jit(solution)/shard_map/reduce_scatter | solution.py:214
  288.8 2.0 select_add_fusion
  (19 shorter events, 0.3 us)
Async XLA Ops:
  8.1 3.7 %collective-permute-start = (bf16[96,512]{1,0:T(8,128)(2,1)S(1)}, bf16[96,512]{1,0:T(8,128)(2,1)S(1)}, u32[]{:S(2)}, u32[]{:S(2)}) collective-permute-start(bf16[96,512]{1,0:T(8,128)(2,1)S(1)} %slice.6), channel_id=1, source_target_pairs={{0,8},{8,16},{16,24},{24,32},{32,40},{40,48},{48,56},{56,64},{64,7... | collective-permute-start | bytes 294920 | tf_op jit(solution)/shard_map/ppermute | solution.py:183
  11.8 1.0 copy-start
  16.5 58.6 %all-to-all-start = ((bf16[8,512,512]{1,2,0:T(8,128)(2,1)}), bf16[8,512,512]{1,2,0:T(8,128)(2,1)}, u32[]{:S(2)}, u32[]{:S(2)}) async-start(bf16[8,512,512]{1,2,0:T(8,128)(2,1)} %broadcast_in_dim.80), calls=%async_computation | async-start | bytes 8388608 | tf_op jit(solution)/shard_map/all_to_all | solution.py:23
  25.0 154.3 %reduce-scatter.5.cloned.1.call-start = ((), (), s32[]{:S(2)}) async-start(), calls=%async_computation.7 | async-start | bytes 2228224 | tf_op jit(solution)/shard_map/reduce_scatter | solution.py:207
  86.7 202.0 %reduce-scatter.3.cloned.1.call-start = ((), (), s32[]{:S(2)}) async-start(), calls=%async_computation.6 | async-start | bytes 8912896 | tf_op jit(solution)/shard_map/reduce_scatter | solution.py:214
  94.5 6.6 %copy-start.1 = (f32[4096]{0:T(1024)S(1)}, f32[4096]{0:T(1024)}, u32[]{:S(2)}) copy-start(f32[4096]{0:T(1024)} %param.10) | copy-start | bytes 49156
  95.9 17.4 %all-to-all-start.2 = ((f32[16,64,128]{2,1,0:T(8,128)}), f32[16,64,128]{2,1,0:T(8,128)S(1)}, u32[]{:S(2)}, u32[]{:S(2)}) async-start(f32[16,64,128]{2,1,0:T(8,128)} %bitcast.9), calls=%async_computation.4 | async-start | bytes 1048576 | tf_op jit(solution)/shard_map/all_to_all | solution.py:194
  115.9 64.7 %all-to-all-start.3 = ((f32[128,64,128]{2,1,0:T(8,128)}), f32[128,64,128]{2,1,0:T(8,128)}, u32[]{:S(2)}, u32[]{:S(2)}) async-start(f32[128,64,128]{2,1,0:T(8,128)} %broadcast_in_dim.90), calls=%async_computation.5 | async-start | bytes 8388608 | tf_op jit(solution)/shard_map/all_to_all | solution.py:23
  181.7 79.8 %all-to-all-start.1 = ((f32[8,256,128]{2,1,0:T(8,128)}), f32[8,256,128]{2,1,0:T(8,128)S(1)}, u32[]{:S(2)}, u32[]{:S(2)}) async-start(f32[8,256,128]{2,1,0:T(8,128)} %broadcast_in_dim.87), calls=%async_computation.3 | async-start | bytes 2097152 | tf_op jit(solution)/shard_map/all_to_all | solution.py:23
Sparse Core Ops, SparseCore 0:
  86.9 92.3 reduce-scatter.4
  181.7 107.0 reduce-scatter.2
